TPU v7x, 32 devices: a whole 2x2x4 slice. The times are simulated.
32 devices in a mesh: dp: 4 (over y, x), ctx: 8 (over z, core).
Axes of the slice: x: 2, y: 2, z: 4, core: 2. Of those that a mesh axis runs over, the one named last changes fastest.
Arguments:
- residual: bfloat16 [4, 1024, 4096], P('dp', 'ctx'), may hold values from -6 to 6
- queries: bfloat16 [4, 1024, 512], P('dp', 'ctx'), may hold values from -6 to 6
- keys_values: bfloat16 [4, 1024, 256], P('dp', 'ctx'), may hold values from -6 to 6
- out_grad: bfloat16 [4, 1024, 512], P('dp', 'ctx'), may hold values from -12 to 12
- w_out: bfloat16 [512, 4096], replicated, may hold values from -0.25 to 0.25
- norm_gain: float32 [4096], replicated, may hold values from 0.5 to 2
- w_router: bfloat16 [4096, 32], replicated, may hold values from -0.09375 to 0.09375
- expert_ids: int32 [4, 1024, 8], P('dp', 'ctx'), may hold values from 0 to 31, all different within a row; in each aligned block of 128 rows (0 to 127, 128 to 255, ..., all dimensions but the last counted through in order) at most 34 rows name the same one
- w_gate_up: bfloat16 [32, 4096, 1536], P(('dp', 'ctx')), may hold values from -0.09375 to 0.09375
- w_down: bfloat16 [32, 768, 4096], P(('dp', 'ctx')), may hold values from -0.21875 to 0.21875
Outputs:
- layer_out: bfloat16 [4, 1024, 4096], P('dp', 'ctx')
- query_grad: bfloat16 [4, 1024, 512], P('dp', 'ctx')
- pair_grad: float32 [4, 1024, 256], P('dp', 'ctx')
Inputs may be any that keep to these rules, and one draw needn't show every extreme that they name: `expert_ids`: within the 128 tokens of one device (aligned blocks of tokens, sequences in order), no expert is named by more than 34 of the choices, a bound that some block reaches. The 8 experts of a token differ.
All inputs are finite; a program needn't handle non-finite values.
Results may differ from a plain program's by a relative error of at most 0.03.
Values may be sent and summed in bfloat16 or wider, within the bound.
A program may use at most 192 MiB of HBM per device.

v0:
```python
import jax
import jax.numpy as jnp
from jax import lax
from jax.sharding import PartitionSpec as P

D = 4096
HD = 128
TOPK = 8
HQ = 4


norm_eps = 1e-06


def expert_block(arrived, w_gate_up, w_down):
    hidden_width = w_down.shape[1]
    gate_up = jnp.einsum("sjid,jdf->sjif", arrived, w_gate_up, preferred_element_type=jnp.float32)
    active = (jax.nn.silu(gate_up[..., :hidden_width]) * gate_up[..., hidden_width:]).astype(
        jnp.bfloat16
    )
    return jnp.einsum("sjif,jfd->sjid", active, w_down, preferred_element_type=jnp.float32).astype(
        jnp.bfloat16
    )


def shards(
    residual,
    queries,
    keys_values,
    out_grad,
    w_out,
    norm_gain,
    w_router,
    expert_ids,
    w_gate_up,
    w_down,
):
    tokens_dev = queries.shape[1]
    row_count = tokens_dev * HQ
    factor = HD ** (-0.5)
    head_rows = queries.reshape(row_count, HD)
    grad_rows = out_grad.reshape(row_count, HD)
    whole_pairs = lax.all_gather(keys_values, "ctx", axis=1, tiled=True)
    length = whole_pairs.shape[1]
    key_rows = whole_pairs[0, :, :HD]
    value_rows = whole_pairs[0, :, HD:]
    offset = lax.axis_index("ctx") * tokens_dev
    query_pos = offset + jnp.arange(row_count, dtype=jnp.int32) // HQ
    key_pos = jnp.arange(length, dtype=jnp.int32)
    causal = key_pos[None, :] <= query_pos[:, None]
    scores = (
        jnp.einsum("rd,kd->rk", head_rows, key_rows, preferred_element_type=jnp.float32) * factor
    )
    scores = jnp.where(causal, scores, -jnp.inf)
    highest = jnp.max(scores, axis=1, keepdims=True)
    weights = jnp.exp(scores - highest)
    totals = jnp.sum(weights, axis=1, keepdims=True)
    attn_probs = weights / totals
    probs_low = attn_probs.astype(jnp.bfloat16)
    attended = jnp.dot(probs_low, value_rows, preferred_element_type=jnp.float32).astype(
        jnp.bfloat16
    )
    row_dot = jnp.sum(
        grad_rows.astype(jnp.float32) * attended.astype(jnp.float32), axis=1, keepdims=True
    )
    prob_grad = jnp.einsum("rd,kd->rk", grad_rows, value_rows, preferred_element_type=jnp.float32)
    score_grad = (attn_probs * (prob_grad - row_dot)).astype(jnp.bfloat16)
    query_grad = (
        jnp.dot(score_grad, key_rows, preferred_element_type=jnp.float32) * factor
    ).astype(jnp.bfloat16)
    key_part = (
        jnp.einsum("rk,rd->kd", score_grad, head_rows, preferred_element_type=jnp.float32) * factor
    )
    value_part = jnp.einsum("rk,rd->kd", probs_low, grad_rows, preferred_element_type=jnp.float32)
    pair_grad = lax.psum_scatter(
        jnp.concatenate([key_part, value_part], axis=1).astype(jnp.bfloat16),
        "ctx",
        scatter_dimension=0,
        tiled=True,
    ).astype(jnp.float32)
    hidden = residual.reshape(tokens_dev, D).astype(jnp.float32) + jnp.dot(
        attended.reshape(tokens_dev, HQ * HD), w_out, preferred_element_type=jnp.float32
    )
    normed = (
        hidden * lax.rsqrt(jnp.mean(hidden * hidden, axis=1, keepdims=True) + norm_eps) * norm_gain
    ).astype(jnp.bfloat16)
    logits = jnp.dot(normed, w_router, preferred_element_type=jnp.float32)
    experts_all = w_router.shape[1]
    routed = expert_ids.reshape(tokens_dev, TOPK)
    route_match = routed[:, :, None] == jnp.arange(experts_all, dtype=jnp.int32)[None, None, :]
    chosen = jnp.sum(jnp.where(route_match, logits[:, None, :], 0.0), axis=2)
    gate_values = jax.nn.sigmoid(chosen)
    mixing = gate_values / jnp.sum(gate_values, axis=1, keepdims=True)
    capacity = tokens_dev * TOPK // experts_all + 2
    onehot = route_match.reshape(tokens_dev * TOPK, experts_all).astype(jnp.int32)
    before = jnp.cumsum(onehot, axis=0) - onehot
    ranked = jnp.sum(before * onehot, axis=1)
    slot_index = routed.reshape(-1) * capacity + ranked
    repeated = jnp.repeat(normed, TOPK, axis=0)
    outgoing = jnp.zeros((experts_all * capacity, D), jnp.bfloat16).at[slot_index].set(repeated)
    dp_size = lax.axis_size("dp")
    ctx_size = lax.axis_size("ctx")
    per_dev = w_gate_up.shape[0]
    returned = lax.all_to_all(
        expert_block(
            lax.all_to_all(
                outgoing.reshape(dp_size * ctx_size, per_dev, capacity, D),
                ("dp", "ctx"),
                split_axis=0,
                concat_axis=0,
                tiled=True,
            ),
            w_gate_up,
            w_down,
        ),
        ("dp", "ctx"),
        split_axis=0,
        concat_axis=0,
        tiled=True,
    )
    results = returned.reshape(experts_all * capacity, D)[slot_index]
    mixture = jnp.einsum(
        "tk,tkd->td", mixing, results.reshape(tokens_dev, TOPK, D).astype(jnp.float32)
    )
    layer_out = (hidden + mixture).astype(jnp.bfloat16).reshape(1, tokens_dev, D)
    return (
        layer_out,
        query_grad.reshape(1, tokens_dev, HQ * HD),
        pair_grad.reshape(1, tokens_dev, 2 * HD),
    )


def solution(mesh):
    placed = (
        P("dp", "ctx", None),
        P("dp", "ctx", None),
        P("dp", "ctx", None),
        P("dp", "ctx", None),
        P(),
        P(),
        P(),
        P("dp", "ctx", None),
        P(("dp", "ctx"), None, None),
        P(("dp", "ctx"), None, None),
    )
    return jax.shard_map(
        shards,
        mesh=mesh,
        in_specs=placed,
        out_specs=(P("dp", "ctx", None), P("dp", "ctx", None), P("dp", "ctx", None)),
        check_vma=False,
    )
```

profile of v0, /device:TPU:0, one launch (start us, length us, event | category | flops | bytes accessed | tf_op | source)
XLA Modules:
  0.0 626.3 jit_solution(10447289645987307145)
XLA Ops:
  7.2 0.7 broadcast_multiply_fusion
  7.9 0.8 copy.40
  9.1 1.0 reshape.143
  10.1 1.0 reshape.131
  11.1 0.8 copy.46
  11.9 9.0 %reduce-window.6 = s32[32,8,128]{2,1,0:T(8,128)S(1)} reduce-window(s32[32,8,128]{2,1,0:T(8,128)S(1)} %fusion.29, s32[]{:T(128)} %constant.23.clone.1), window={size=1x1x128 pad=0_0x0_0x127_0}, to_apply=%region_5.6 | reduce-window | flops 4161536 | bytes 262148 | tf_op jit(solution)/shard_map/reduce-window
  21.2 0.8 broadcast_add_fusion
  22.0 16.8 %all_gather.3 = bf16[1,1024,256]{2,1,0:T(8,128)(2,1)S(1)} all-gather(bf16[1,128,256]{2,1,0:T(8,128)(2,1)} %param.12), channel_id=1, replica_groups=mesh['dp'=4,'ctx'=8] {'ctx'}, dimensions={1}, use_global_device_ids=true | all-gather | bytes 589824 | tf_op jit(solution)/shard_map/all_gather | solution.py:43
  40.4 1.2 multiply_reduce_fusion.1
  41.5 1.7 copy.38
  43.2 1.6 reshape.132
  44.9 3.2 multiply_reduce_fusion
  48.2 1.2 copy-done.1
  49.7 16.3 %scatter_custom_fusion = bf16[1088,4096]{1,0:T(8,128)(2,1)} fusion(s32[1024]{0:T(1024)S(1)} %bitcast.106, bf16[]{:T(256)} %constant.50.clone.1, bf16[128,4096]{1,0:T(8,128)(2,1)S(1)} %multiply_convert_fusion.1), kind=kCustom, calls=%fused_computation.8 | custom fusion | bytes 9961474 | tf_op jit(solution)/shard_map/scatter | solution.py:100
  66.0 10.3 %reshape.135 = bf16[32,1,34,4096]{3,2,0,1:T(8,128)(2,1)} reshape(bf16[1088,4096]{1,0:T(8,128)(2,1)} %scatter_custom_fusion) | data formatting | bytes 17825792 | tf_op jit(solution)/shard_map/reshape | solution.py:107
  76.4 235.4 %all_to_all.10 = bf16[32,1,34,4096]{3,2,1,0:T(8,128)(2,1)S(1)} all-to-all(bf16[32,1,34,4096]{3,2,1,0:T(8,128)(2,1)} %bitcast.101), channel_id=1, replica_groups=mesh['dp'=4,'ctx'=8] {'dp','ctx'}, dimensions={0} | all-to-all | bytes 17825792 | tf_op jit(solution)/shard_map/all_to_all | solution.py:106
  311.8 19.8 %fusion.8 = f32[32,1,34,1536]{3,2,0,1:T(8,128)S(1)} fusion(bf16[1,4096,1536]{2,1,0:T(8,128)(2,1)} %param.18, bf16[32,1,34,4096]{3,2,1,0:T(8,128)(2,1)S(1)} %all_to_all.10), kind=kOutput, calls=%fused_computation.12 | convolution fusion | flops 13690208256 | bytes 28180480 | tf_op jit(solution)/shard_map/sjid,jdf->sjif/dot_general | solution.py:17
  331.6 11.2 %convert_bitcast_fusion = bf16[32,1,34,4096]{3,2,1,0:T(8,128)(2,1)} fusion(bf16[1,768,4096]{2,1,0:T(8,128)(2,1)S(1)} %bitcast.109, f32[32,1,34,1536]{3,2,0,1:T(8,128)S(1)} %fusion.8), kind=kOutput, calls=%fused_computation.5 | convolution fusion | flops 6854574080 | bytes 21889024 | tf_op jit(solution)/shard_map/sjif,jfd->sjid/dot_general | solution.py:21
  342.8 3.7 all-to-all-start.1
  346.8 1.4 multiply_convert_fusion
  348.2 1.4 fusion.21
  350.0 1.0 copy.50
  351.0 1.7 fusion.22
  352.8 0.7 reshape.144
  354.2 37.0 %reduce-scatter.4.cloned.1.call-done = bf16[128,256]{1,0:T(8,128)(2,1)} async-done(((bf16[1024,256]{1,0:T(8,128)(2,1)}), bf16[128,256]{1,0:T(8,128)(2,1)}) %reduce-scatter.4.cloned.1.call-update) | async-done | bytes 65552
  391.2 0.9 copy.51
  392.2 0.8 copy.47
  393.0 188.3 %all-to-all-done.1 = bf16[32,1,34,4096]{3,2,1,0:T(8,128)(2,1)} async-done(((bf16[32,1,34,4096]{3,2,1,0:T(8,128)(2,1)}), bf16[32,1,34,4096]{3,2,1,0:T(8,128)(2,1)}, u32[]{:S(2)}, u32[]{:S(2)}) %all-to-all-start.1) | async-done | bytes 8912928 | tf_op jit(solution)/shard_map/all_to_all | solution.py:104
  581.3 10.4 %reshape.140 = bf16[1088,4096]{1,0:T(8,128)(2,1)} reshape(bf16[32,1,34,4096]{3,2,1,0:T(8,128)(2,1)} %all-to-all-done.1) | data formatting | bytes 17825792 | tf_op jit(solution)/shard_map/reshape | solution.py:121
  591.7 19.7 %gather_fusion = bf16[1024,4096]{1,0:T(8,128)(2,1)} fusion(bf16[1088,4096]{1,0:T(8,128)(2,1)} %reshape.140, s32[1024]{0:T(1024)S(1)} %broadcast_clamp_fusion), kind=kCustom, calls=%fused_computation | custom fusion | bytes 16781312 | tf_op jit(solution)/shard_map/gather | solution.py:121
  611.5 5.8 fusion.3
  617.3 2.2 fusion.23
  (55 shorter events, 4.0 us)
Async XLA Ops:
  7.2 346.3 %copy-start = (bf16[4096,32]{0,1:T(8,128)(2,1)S(1)}, bf16[4096,32]{0,1:T(8,128)(2,1)}, u32[]{:S(2)}) copy-start(bf16[4096,32]{0,1:T(8,128)(2,1)} %param.16) | copy-start | bytes 786436
  11.1 28.2 %copy-start.8 = (bf16[512,128]{1,0:T(8,128)(2,1)}, bf16[512,128]{1,0:T(8,128)(2,1)S(1)}, u32[]{:S(2)}) copy-start(bf16[512,128]{1,0:T(8,128)(2,1)S(1)} %reshape.131) | copy-start | bytes 393220
  38.8 1.6 copy-start.4
  38.8 1.6 copy-start.6
  39.9 5.0 copy-start.5
  44.9 3.2 copy-start.7
  44.9 4.6 copy-start.10
  48.1 1.3 copy-start.1
  76.4 255.2 %slice-start = ((s8[6291456]{0:T(1024)(128)(4,1)}), s8[4194304]{0:T(1024)(128)(4,1)S(1)}, s32[]{:S(2)}) async-start(s8[6291456]{0:T(1024)(128)(4,1)} %bitcast.108), calls=%async_computation.4 | async-start | bytes 8388608
  311.8 19.8 %slice-start.1 = ((s8[6291456]{0:T(1024)(128)(4,1)}), s8[2097152]{0:T(1024)(128)(4,1)S(1)}, s32[]{:S(2)}) async-start(s8[6291456]{0:T(1024)(128)(4,1)} %bitcast.108), calls=%async_computation.5 | async-start | bytes 4194304
  342.8 238.5 %all-to-all-start.1 = ((bf16[32,1,34,4096]{3,2,1,0:T(8,128)(2,1)}), bf16[32,1,34,4096]{3,2,1,0:T(8,128)(2,1)}, u32[]{:S(2)}, u32[]{:S(2)}) async-start(bf16[32,1,34,4096]{3,2,1,0:T(8,128)(2,1)} %convert_bitcast_fusion), calls=%async_computation.1 | async-start | bytes 20971520 | tf_op jit(solution)/shard_map/all_to_all | solution.py:104
  346.5 44.8 %reduce-scatter.4.cloned.1.call-start = ((), (), s32[]{:S(2)}) async-start(), calls=%async_computation.3 | async-start | bytes 589824
  348.2 1.8 copy-start.3
  349.6 4.4 copy-start.9
  611.4 5.8 copy-start.2
Sparse Core Ops, SparseCore 0:
  351.2 40.0 reduce-scatter.3
where the time goes:
time: 627 us; the launch traced here: 626 us
  blocking collectives  252 us (40%)
  waiting for transfers between devices  225 us (36%)
  local copies, waits for them, and re-layouts  69.3 us (11%)
  matrix products  47 us (7%)
  between operations  14.3 us (2%)
  other arithmetic  14.2 us (2%)
    all_to_all x1, blocking collectives, shards(): lax.all_to_all(outgoing.reshape(dp_size * ctx_size, per_dev, capacity, D)...  235 us
    all_to_all x1, waiting for transfers between devices, shards(): lax.all_to_all(expert_block(lax.all_to_all(outgoing.reshape(dp_size * ctx...  188 us
    unnamed x2, waiting for transfers between devices  37.1 us
    dot_general x1, matrix products, expert_block(): jnp.einsum('sjid,jdf->sjif', arrived, w_gate_up, preferred_element_type=j...  19.8 us
    gather x1, local copies, waits for them, and re-layouts, shards(): results = returned.reshape(experts_all * capacity, D)[slot_index]  19.7 us
    all_gather x1, blocking collectives, shards(): whole_pairs = lax.all_gather(keys_values, 'ctx', axis=1, tiled=True)  16.8 us
    scatter x1, local copies, waits for them, and re-layouts, shards(): jnp.zeros((experts_all * capacity, D), jnp.bfloat16).at[slot_index]  16.3 us
  transfers between devices with their start and end apart: 2, of which 2 were waited for; matrix products, arithmetic and copies ran while one was open for 1% of the time, Pallas kernels for 0%

commit v1 on v0

--- a/solution.py
+++ b/solution.py
@@ -21,6 +21,84 @@
     return jnp.einsum("sjif,jfd->sjid", active, w_down, preferred_element_type=jnp.float32).astype(
         jnp.bfloat16
     )
+
+
+def exchange_mixture(normed, routed, mixing, route_match, w_gate_up, w_down):
+    tokens_dev, experts_all = normed.shape[0], route_match.shape[2]
+    capacity = tokens_dev * TOPK // experts_all + 2
+    onehot = route_match.reshape(tokens_dev * TOPK, experts_all).astype(jnp.int32)
+    before = jnp.cumsum(onehot, axis=0) - onehot
+    ranked = jnp.sum(before * onehot, axis=1)
+    slot_index = routed.reshape(-1) * capacity + ranked
+    repeated = jnp.repeat(normed, TOPK, axis=0)
+    outgoing = jnp.zeros((experts_all * capacity, D), jnp.bfloat16).at[slot_index].set(repeated)
+    dp_size = lax.axis_size("dp")
+    ctx_size = lax.axis_size("ctx")
+    per_dev = w_gate_up.shape[0]
+    returned = lax.all_to_all(
+        expert_block(
+            lax.all_to_all(
+                outgoing.reshape(dp_size * ctx_size, per_dev, capacity, D),
+                ("dp", "ctx"),
+                split_axis=0,
+                concat_axis=0,
+                tiled=True,
+            ),
+            w_gate_up,
+            w_down,
+        ),
+        ("dp", "ctx"),
+        split_axis=0,
+        concat_axis=0,
+        tiled=True,
+    )
+    results = returned.reshape(experts_all * capacity, D)[slot_index]
+    mixture = jnp.einsum(
+        "tk,tkd->td", mixing, results.reshape(tokens_dev, TOPK, D).astype(jnp.float32)
+    )
+    return mixture
+
+
+def gathered_mixture(normed, dense_mix, w_gate_up, w_down):
+    tokens_dev, experts_all = dense_mix.shape
+    hidden_width = w_down.shape[1]
+    axes = ("dp", "ctx")
+    blocks = lax.axis_size("dp") * lax.axis_size("ctx")
+    capacity = tokens_dev * TOPK // experts_all + 2
+    group = 4
+    groups, group_rows, group_cap = blocks // group, group * tokens_dev, group * capacity
+    rows_all = lax.all_gather(normed, axes, axis=0, tiled=True)
+    weights = lax.all_to_all(
+        dense_mix.T.reshape(experts_all, 1, tokens_dev), axes, split_axis=0, concat_axis=0, tiled=True
+    ).reshape(groups, group_rows)
+    named = weights != 0.0
+    rank = jnp.cumsum(named.astype(jnp.int32), axis=1) - 1
+    slots = jnp.arange(group_cap, dtype=jnp.int32)
+    pick = (rank[:, None, :] == slots[None, :, None]) & named[:, None, :]
+    slot_weight = jnp.sum(jnp.where(pick, weights[:, None, :], 0.0), axis=2)
+    pick = pick.astype(jnp.bfloat16)
+    arrived = jnp.einsum(
+        "gct,gtd->gcd",
+        pick,
+        rows_all.reshape(groups, group_rows, D),
+        preferred_element_type=jnp.float32,
+    ).astype(jnp.bfloat16)
+    arrived = arrived.reshape(groups * group_cap, D)
+    gate_up = jnp.dot(arrived, w_gate_up[0], preferred_element_type=jnp.float32)
+    active = (jax.nn.silu(gate_up[:, :hidden_width]) * gate_up[:, hidden_width:]).astype(
+        jnp.bfloat16
+    )
+    outs = jnp.dot(active, w_down[0], preferred_element_type=jnp.float32).astype(jnp.bfloat16)
+    outs = (outs.astype(jnp.float32) * slot_weight.reshape(-1, 1)).astype(jnp.bfloat16)
+    part = jnp.einsum(
+        "gct,gcd->gtd",
+        pick,
+        outs.reshape(groups, group_cap, D),
+        preferred_element_type=jnp.float32,
+    ).astype(jnp.bfloat16)
+    return lax.psum_scatter(
+        part.reshape(blocks * tokens_dev, D), axes, scatter_dimension=0, tiled=True
+    ).astype(jnp.float32)
 
 
 def shards(
@@ -91,37 +169,11 @@
     chosen = jnp.sum(jnp.where(route_match, logits[:, None, :], 0.0), axis=2)
     gate_values = jax.nn.sigmoid(chosen)
     mixing = gate_values / jnp.sum(gate_values, axis=1, keepdims=True)
-    capacity = tokens_dev * TOPK // experts_all + 2
-    onehot = route_match.reshape(tokens_dev * TOPK, experts_all).astype(jnp.int32)
-    before = jnp.cumsum(onehot, axis=0) - onehot
-    ranked = jnp.sum(before * onehot, axis=1)
-    slot_index = routed.reshape(-1) * capacity + ranked
-    repeated = jnp.repeat(normed, TOPK, axis=0)
-    outgoing = jnp.zeros((experts_all * capacity, D), jnp.bfloat16).at[slot_index].set(repeated)
-    dp_size = lax.axis_size("dp")
-    ctx_size = lax.axis_size("ctx")
-    per_dev = w_gate_up.shape[0]
-    returned = lax.all_to_all(
-        expert_block(
-            lax.all_to_all(
-                outgoing.reshape(dp_size * ctx_size, per_dev, capacity, D),
-                ("dp", "ctx"),
-                split_axis=0,
-                concat_axis=0,
-                tiled=True,
-            ),
-            w_gate_up,
-            w_down,
-        ),
-        ("dp", "ctx"),
-        split_axis=0,
-        concat_axis=0,
-        tiled=True,
-    )
-    results = returned.reshape(experts_all * capacity, D)[slot_index]
-    mixture = jnp.einsum(
-        "tk,tkd->td", mixing, results.reshape(tokens_dev, TOPK, D).astype(jnp.float32)
-    )
+    if experts_all <= 4 * TOPK:
+        dense_mix = jnp.sum(jnp.where(route_match, mixing[:, :, None], 0.0), axis=1)
+        mixture = gathered_mixture(normed, dense_mix, w_gate_up, w_down)
+    else:
+        mixture = exchange_mixture(normed, routed, mixing, route_match, w_gate_up, w_down)
     layer_out = (hidden + mixture).astype(jnp.bfloat16).reshape(1, tokens_dev, D)
     return (
         layer_out,

time: 627 us -> 666 us (1.062)
  waiting for transfers between devices: 225 us -> 538 us
  blocking collectives: 252 us -> 16.8 us
  local copies, waits for them, and re-layouts: 69.3 us -> 12.2 us
  matrix products: 47 us -> 69.3 us
    reduce_scatter x0 -> x1, waiting for transfers between devices: none -> 355 us  [gathered_mixture(): lax.psum_scatter(part.reshape(blocks * tokens_dev, D), axes, scatter_dime...]
    all_to_all x1 -> x0, blocking collectives: 235 us -> none  [shards(): lax.all_to_all(outgoing.reshape(dp_size * ctx_size, per_dev, capacity, D)...]
    all_to_all x1, waiting for transfers between devices: 188 us -> 3.56 us  [gathered_mixture(): lax.all_to_all(dense_mix.T.reshape(experts_all, 1, tokens_dev), axes, spl...]
    all_gather x0 -> x1, waiting for transfers between devices: none -> 179 us  [gathered_mixture(): rows_all = lax.all_gather(normed, axes, axis=0, tiled=True)]
    unnamed x2 -> x4, waiting for transfers between devices: 37.1 us -> 0.05 us
    dot_general x3 -> x4, matrix products: 36.8 us -> 58.5 us  [the longest x1 17.3 us: gathered_mixture(): gate_up = jnp.dot(arrived, w_gate_up[0], preferred_element_type=jnp.float32)]
    reshape x2 -> x1, local copies, waits for them, and re-layouts: 20.8 us -> 0.01 us  [gathered_mixture(): weights = lax.all_to_all(dense_mix.T.reshape(experts_all, 1, tokens_dev),...]
    gather x1 -> x0, local copies, waits for them, and re-layouts: 19.7 us -> none  [shards(): results = returned.reshape(experts_all * capacity, D)[slot_index]]
  transfers between devices with their start and end apart: 2 -> 4, of which waited for: 2 -> 3; matrix products, arithmetic and copies ran while one was open for 1% -> 11% of each run, Pallas kernels for 0% -> 0%
where the time goes in v1:
time: 666 us
  waiting for transfers between devices  538 us (81%)
  matrix products  69.3 us (10%)
  blocking collectives  16.8 us (3%)
  between operations  15.7 us (2%)
  local copies, waits for them, and re-layouts  12.2 us (2%)
  other arithmetic  7.9 us (1%)
    reduce_scatter x1, waiting for transfers between devices, gathered_mixture(): lax.psum_scatter(part.reshape(blocks * tokens_dev, D), axes, scatter_dime...  355 us
    all_gather x1, waiting for transfers between devices, gathered_mixture(): rows_all = lax.all_gather(normed, axes, axis=0, tiled=True)  179 us
    dot_general x1, matrix products, gathered_mixture(): gate_up = jnp.dot(arrived, w_gate_up[0], preferred_element_type=jnp.float32)  17.3 us
    all_gather x1, blocking collectives, shards(): whole_pairs = lax.all_gather(keys_values, 'ctx', axis=1, tiled=True)  16.8 us
    dot_general x1, matrix products, gathered_mixture(): jnp.einsum('gct,gtd->gcd', pick, rows_all.reshape(groups, group_rows, D),...  16.7 us
    dot_general x1, matrix products, gathered_mixture(): jnp.einsum('gct,gcd->gtd', pick, outs.reshape(groups, group_cap, D), pref...  13.9 us
  transfers between devices with their start and end apart: 4, of which 3 were waited for; matrix products, arithmetic and copies ran while one was open for 11% of the time, Pallas kernels for 0%

profile of v1, /device:TPU:0, one launch (start us, length us, event | category | flops | bytes accessed | tf_op | source)
XLA Modules:
  0.0 665.7 jit_solution(11630965576128566953)
XLA Ops:
  8.1 1.0 reshape.142
  9.1 1.0 reshape.132
  10.1 0.8 copy.33
  10.9 16.8 %all_gather.6 = bf16[1,1024,256]{2,1,0:T(8,128)(2,1)S(1)} all-gather(bf16[1,128,256]{2,1,0:T(8,128)(2,1)} %param.12), channel_id=1, replica_groups=mesh['dp'=4,'ctx'=8] {'ctx'}, dimensions={1}, use_global_device_ids=true | all-gather | bytes 589824 | tf_op jit(solution)/shard_map/all_gather | solution.py:121
  27.7 0.6 fusion.25
  29.7 1.7 multiply_reduce_fusion.1
  31.3 1.7 copy.29
  33.0 1.6 reshape.133
  34.7 3.2 multiply_reduce_fusion
  37.9 1.3 copy-done.2
  39.2 1.3 multiply_convert_fusion.2
  40.5 1.7 fusion.26
  42.3 0.6 select_reduce_fusion.1
  42.9 5.6 all-to-all-start
  48.6 1.4 multiply_convert_fusion.1
  50.8 1.0 copy.35
  52.1 3.6 all-to-all-done
  55.6 0.5 broadcast.109
  56.1 0.7 reduce.5
  56.9 1.1 reduce-window.6
  58.3 0.6 select_reduce_fusion
  59.0 179.2 %all-gather.2.cloned.1.call-done = bf16[4096,4096]{1,0:T(8,128)(2,1)} async-done(((bf16[128,4096]{1,0:T(8,128)(2,1)}), bf16[4096,4096]{1,0:T(8,128)(2,1)}) %all-gather.2.cloned.1.call-update) | async-done | bytes 33554448 | tf_op jit(solution)/shard_map/all_gather | solution.py:70
  238.2 16.7 %convolution_convert_fusion.2 = bf16[8,136,4096]{2,1,0:T(8,128)(2,1)} fusion(bf16[8,512,4096]{2,1,0:T(8,128)(2,1)} %bitcast.55, s32[8,512]{1,0:T(8,128)S(1)} %add_bitcast_fusion, pred[8,512]{1,0:T(8,128)(4,1)S(1)} %broadcast_compare_fusion), kind=kOutput, calls=%fused_computation.5 | convolution fusion | flops 4568973312 | bytes 42487808 | tf_op jit(solution)/shard_map/gct,gtd->gcd/dot_general | solution.py:80
  254.9 17.3 %fusion = f32[1088,1536]{1,0:T(8,128)S(1)} fusion(bf16[1088,4096]{1,0:T(8,128)(2,1)} %bitcast.57, bf16[1,4096,1536]{2,1,0:T(8,128)(2,1)} %param.18), kind=kOutput, calls=%fused_computation.3 | convolution fusion | flops 13690208256 | bytes 28180480 | tf_op jit(solution)/shard_map/dot_general | solution.py:87
  272.2 10.6 %multiply_convert_fusion = bf16[1088,4096]{1,0:T(8,128)(2,1)S(1)} fusion(f32[1088]{0:T(1024)S(1)} %mul.73, bf16[1,768,4096]{2,1,0:T(8,128)(2,1)} %param.19, f32[1088,1536]{1,0:T(8,128)S(1)} %fusion), kind=kOutput, calls=%fused_computation.1 | convolution fusion | flops 6867943424 | bytes 21893376 | tf_op jit(solution)/shard_map/dot_general | solution.py:91
  282.8 13.9 %convolution_convert_fusion = bf16[8,512,4096]{2,1,0:T(8,128)(2,1)} fusion(bf16[8,136,4096]{2,1,0:T(8,128)(2,1)S(1)} %bitcast.56, s32[8,512]{1,0:T(8,128)S(1)} %add_bitcast_fusion, pred[8,512]{1,0:T(8,128)(4,1)S(1)} %broadcast_compare_fusion), kind=kOutput, calls=%fused_computation | convolution fusion | flops 4581294080 | bytes 42487808 | tf_op jit(solution)/shard_map/gct,gcd->gtd/dot_general | solution.py:93
  296.7 1.5 fusion.12
  298.3 0.7 reshape.143
  299.0 0.9 copy.36
  300.0 0.8 copy.34
  300.8 355.1 %reduce-scatter.5.cloned.1.call-done = bf16[128,4096]{1,0:T(8,128)(2,1)} async-done(((bf16[4096,4096]{1,0:T(8,128)(2,1)}), bf16[128,4096]{1,0:T(8,128)(2,1)}) %reduce-scatter.5.cloned.1.call-update) | async-done | bytes 1048592 | tf_op jit(solution)/shard_map/reduce_scatter | solution.py:99
  655.9 2.4 fusion.17
  (48 shorter events, 3.1 us)
Async XLA Ops:
  8.0 32.5 %copy-start = (bf16[4096,32]{0,1:T(8,128)(2,1)S(1)}, bf16[4096,32]{0,1:T(8,128)(2,1)}, u32[]{:S(2)}) copy-start(bf16[4096,32]{0,1:T(8,128)(2,1)} %param.16) | copy-start | bytes 786436
  8.0 230.1 %all-gather.2.cloned.1.call-start = ((), (), s32[]{:S(2)}) async-start(), calls=%async_computation.3 | async-start | bytes 34603008 | tf_op jit(solution)/shard_map/all_gather | solution.py:70
  10.1 18.1 %copy-start.7 = (bf16[512,128]{1,0:T(8,128)(2,1)}, bf16[512,128]{1,0:T(8,128)(2,1)S(1)}, u32[]{:S(2)}) copy-start(bf16[512,128]{1,0:T(8,128)(2,1)S(1)} %reshape.132) | copy-start | bytes 393220
  27.7 1.6 copy-start.4
  28.7 0.9 copy-start.6
  29.7 5.0 copy-start.5
  34.7 4.6 copy-start.9
  37.9 1.4 copy-start.2
  39.2 3.0 copy-start.10
  42.2 7.8 %copy-start.8 = (bf16[512,128]{1,0:T(8,128)(2,1)S(1)}, bf16[512,128]{1,0:T(8,128)(2,1)}, u32[]{:S(2)}) copy-start(bf16[512,128]{1,0:T(8,128)(2,1)} %copy-done.7) | copy-start | bytes 393220
  42.9 12.7 %all-to-all-start = ((f32[32,1,128]{2,1,0:T(1,128)}), f32[32,1,128]{2,1,0:T(1,128)S(1)}, u32[]{:S(2)}, u32[]{:S(2)}) async-start(f32[32,1,128]{2,1,0:T(1,128)} %bitcast.6), calls=%async_computation | async-start | bytes 32768 | tf_op jit(solution)/shard_map/all_to_all | solution.py:71
  48.5 250.5 %reduce-scatter.7.cloned.1.call-start = ((), (), s32[]{:S(2)}) async-start(), calls=%async_computation.5 | async-start | bytes 589824
  51.8 604.1 %reduce-scatter.5.cloned.1.call-start = ((), (), s32[]{:S(2)}) async-start(), calls=%async_computation.4 | async-start | bytes 34603008 | tf_op jit(solution)/shard_map/reduce_scatter | solution.py:99
  296.7 359.2 %copy-start.3 = (f32[128,4096]{1,0:T(8,128)S(1)}, f32[128,4096]{1,0:T(8,128)}, u32[]{:S(2)}) copy-start(f32[128,4096]{1,0:T(8,128)} %copy-done.2) | copy-start | bytes 6291460
  300.0 358.3 %copy-start.1 = (bf16[4096,32]{0,1:T(8,128)(2,1)S(1)}, bf16[4096,32]{0,1:T(8,128)(2,1)}, u32[]{:S(2)}) copy-start(bf16[4096,32]{0,1:T(8,128)(2,1)} %param.16) | copy-start | bytes 786436
Sparse Core Ops, SparseCore 0:
  40.6 197.4 all-gather.1
Sparse Core Ops, SparseCore 1:
  51.9 60.7 reduce-scatter.6
  296.8 359.0 reduce-scatter.4

commit v2 on v1

--- a/solution.py
+++ b/solution.py
@@ -1,6 +1,10 @@
+import functools
+
 import jax
 import jax.numpy as jnp
 from jax import lax
+from jax.experimental import pallas as pl
+from jax.experimental.pallas import tpu as pltpu
 from jax.sharding import PartitionSpec as P
 
 D = 4096
@@ -59,6 +63,372 @@
     return mixture
 
 
+MESH = pl.DeviceIdType.MESH
+
+
+class Place:
+    def __init__(self, depth):
+        self.depth = depth
+        self.dp = lax.axis_index("dp")
+        ctx = lax.axis_index("ctx")
+        self.z, self.core = ctx // 2, ctx % 2
+        x_flip = (self.dp // 2) * 2 + 1 - self.dp % 2
+        y_flip = (self.dp + 2) % 4
+        self.near_dp = x_flip * (1 - self.core) + y_flip * self.core
+        self.far_dp = y_flip * (1 - self.core) + x_flip * self.core
+        self.both_dp = 3 - self.dp
+        self.near = (self.near_dp, ctx)
+        self.far = (self.far_dp, ctx)
+        self.other_core = (self.dp, self.z * 2 + 1 - self.core)
+        self.up = (self.dp, ctx + 2)
+        self.down = (self.dp, ctx - 2)
+        self.has_up = self.z < depth - 1
+        self.has_down = self.z > 0
+
+    def block(self, dp, z, core=None):
+        return (dp * self.depth + z) * 2 + (self.core if core is None else core)
+
+    def greet(self):
+        barrier = pltpu.get_barrier_semaphore()
+        for target in (self.near, self.far, self.other_core):
+            pl.semaphore_signal(barrier, inc=1, device_id=target, device_id_type=MESH)
+
+        @pl.when(self.has_up)
+        def _():
+            pl.semaphore_signal(barrier, inc=1, device_id=self.up, device_id_type=MESH)
+
+        @pl.when(self.has_down)
+        def _():
+            pl.semaphore_signal(barrier, inc=1, device_id=self.down, device_id_type=MESH)
+
+        pl.semaphore_wait(
+            barrier, 3 + self.has_up.astype(jnp.int32) + self.has_down.astype(jnp.int32)
+        )
+
+
+def gather_kernel(depth, rows_ref, all_ref, own_sem, send_sem, recv_sem):
+    place = Place(depth)
+    z = place.z
+    targets = (place.near, place.far, place.other_core, place.up, place.down)
+    NEAR, FAR, CORE, UP, DOWN = range(5)
+    own = place.block(place.dp, z)
+
+    def copy(kind, block, source=None):
+        return pltpu.make_async_remote_copy(
+            src_ref=all_ref.at[block] if source is None else source,
+            dst_ref=all_ref.at[block],
+            send_sem=send_sem.at[kind, block],
+            recv_sem=recv_sem.at[block],
+            device_id=targets[kind],
+            device_id_type=MESH,
+        )
+
+    def along(distance):
+        if distance == 0:
+            return [(z, None, None)]
+        return [(z - distance, z >= distance, UP), (z + distance, z + distance < depth, DOWN)]
+
+    def run(condition, body):
+        if condition is None:
+            body()
+        else:
+            pl.when(condition)(body)
+
+    own_copy = pltpu.make_async_copy(rows_ref, all_ref.at[own], own_sem)
+    place.greet()
+    own_copy.start()
+    pl.when(place.has_up)(lambda: copy(UP, own, rows_ref).start())
+    pl.when(place.has_down)(lambda: copy(DOWN, own, rows_ref).start())
+    for kind in (FAR, NEAR, CORE):
+        copy(kind, own, rows_ref).start()
+
+    def from_line(distance):
+        for source, condition, onward in along(distance):
+
+            def body(source=source, onward=onward):
+                block = place.block(place.dp, source)
+                copy(onward, block).wait_recv()
+                more = place.has_up if onward == UP else place.has_down
+                pl.when(more)(lambda: copy(onward, block).start())
+                for kind in (NEAR, FAR, CORE):
+                    copy(kind, block).start()
+
+            run(condition, body)
+
+    def from_near(distance):
+        for source, condition, _ in along(distance):
+
+            def body(source=source):
+                block = place.block(place.near_dp, source)
+                copy(NEAR, block).wait_recv()
+                for kind in (FAR, CORE):
+                    copy(kind, block).start()
+
+            run(condition, body)
+
+    def from_far(distance):
+        for source, condition, _ in along(distance):
+
+            def body(source=source):
+                for dp in (place.far_dp, place.both_dp):
+                    block = place.block(dp, source)
+                    copy(FAR, block).wait_recv()
+                    copy(CORE, block).start()
+
+            run(condition, body)
+
+    for distance in range(depth):
+        if distance:
+            from_line(distance)
+        from_near(distance)
+        if distance:
+            from_far(distance - 1)
+    from_far(depth - 1)
+
+    for dp in range(4):
+        for level in range(depth):
+            copy(CORE, place.block(dp, level, 1 - place.core)).wait_recv()
+    own_copy.wait()
+    for distance in range(depth):
+        for source, condition, onward in along(distance):
+
+            def body(source=source, onward=onward):
+                block = place.block(place.dp, source)
+                for kind in (NEAR, FAR, CORE):
+                    copy(kind, block).wait_send()
+                if onward != DOWN:
+                    pl.when(place.has_up)(lambda: copy(UP, block).wait_send())
+                if onward != UP:
+                    pl.when(place.has_down)(lambda: copy(DOWN, block).wait_send())
+                block = place.block(place.near_dp, source)
+                for kind in (FAR, CORE):
+                    copy(kind, block).wait_send()
+                for dp in (place.far_dp, place.both_dp):
+                    copy(CORE, place.block(dp, source)).wait_send()
+
+            run(condition, body)
+
+
+def gather_rows(rows, depth):
+    tokens_dev, width = rows.shape
+    blocks = 8 * depth
+    return pl.pallas_call(
+        functools.partial(gather_kernel, depth),
+        out_shape=jax.ShapeDtypeStruct((blocks, tokens_dev, width), rows.dtype),
+        in_specs=[pl.BlockSpec(memory_space=pl.ANY)],
+        out_specs=pl.BlockSpec(memory_space=pl.ANY),
+        scratch_shapes=[
+            pltpu.SemaphoreType.DMA(()),
+            pltpu.SemaphoreType.DMA((5, blocks)),
+            pltpu.SemaphoreType.DMA((blocks,)),
+        ],
+        compiler_params=pltpu.CompilerParams(collective_id=1, has_side_effects=True),
+    )(rows)
+
+
+def reduce_kernel(
+    depth,
+    part_ref,
+    out_ref,
+    total,
+    core_in,
+    far_in,
+    near_in,
+    line_in,
+    own_sem,
+    core_send,
+    core_recv,
+    far_send,
+    far_recv,
+    near_send,
+    near_recv,
+    line_send,
+    line_recv,
+):
+    place = Place(depth)
+    z = place.z
+    rows = out_ref.shape[0]
+
+    def order(i):
+        falling = lambda at: jnp.where(
+            depth - 1 - i > at, depth - 1 - i, depth - 2 - i if i < depth - 1 else at
+        )
+        return jnp.where(z < depth // 2, falling(z), depth - 1 - falling(depth - 1 - z))
+
+    levels = [order(i) for i in range(depth)]
+
+    def add(into, term):
+        def step(i, carry):
+            at = pl.ds(pl.multiple_of(i * 16, 16), 16)
+            into[at, :] = (
+                into[at, :].astype(jnp.float32) + term[at, :].astype(jnp.float32)
+            ).astype(jnp.bfloat16)
+            return carry
+
+        lax.fori_loop(0, rows // 16, step, 0)
+
+    def remote(source, into, send, recv, target):
+        return pltpu.make_async_remote_copy(
+            src_ref=source,
+            dst_ref=into,
+            send_sem=send,
+            recv_sem=recv,
+            device_id=target,
+            device_id_type=MESH,
+        )
+
+    def slot(dp, level):
+        return dp * depth + level
+
+    def load(dp, level):
+        at = slot(dp, level)
+        return pltpu.make_async_copy(
+            part_ref.at[place.block(dp, level)], total.at[at], own_sem.at[at]
+        )
+
+    def to_core(dp, level):
+        at = slot(dp, level)
+        return remote(
+            part_ref.at[place.block(dp, level, 1 - place.core)],
+            core_in.at[at],
+            core_send.at[at],
+            core_recv.at[at],
+            place.other_core,
+        )
+
+    def to_far(side, dp, level):
+        at = side * depth + level
+        return remote(
+            total.at[slot(dp, level)], far_in.at[at], far_send.at[at], far_recv.at[at], place.far
+        )
+
+    def to_near(level):
+        return remote(
+            total.at[slot(place.near_dp, level)],
+            near_in.at[level],
+            near_send.at[level],
+            near_recv.at[level],
+            place.near,
+        )
+
+    def to_line(level, at, target):
+        return remote(
+            total.at[slot(place.dp, level)],
+            line_in.at[at],
+            line_send.at[level],
+            line_recv.at[at],
+            target,
+        )
+
+    place.greet()
+    theirs = (place.both_dp, place.near_dp, place.far_dp, place.dp)
+    mine = (place.both_dp, place.far_dp, place.near_dp, place.dp)
+    for dp in range(4):
+        for level in levels:
+            to_core(theirs[dp], level).start()
+            load(mine[dp], level).start()
+    for turn, dp in enumerate(mine):
+        for level in levels:
+            at = slot(dp, level)
+            load(dp, level).wait()
+            to_core(dp, level).wait_recv()
+            add(total.at[at], core_in.at[at])
+            if turn < 2:
+                to_far(1 - turn, dp, level).start()
+    for level in levels:
+        at = slot(place.near_dp, level)
+        to_far(1, place.both_dp, level).wait_recv()
+        add(total.at[at], far_in.at[depth + level])
+        to_near(level).start()
+    for level in levels:
+        at = slot(place.dp, level)
+        to_far(0, place.far_dp, level).wait_recv()
+        add(total.at[at], far_in.at[level])
+        to_near(level).wait_recv()
+        add(total.at[at], near_in.at[level])
+
+        @pl.when(level > z)
+        def _():
+            @pl.when(place.has_down)
+            def _():
+                to_line(level, level, place.up).wait_recv()
+                add(total.at[at], line_in.at[level])
+
+            to_line(level, level, place.up).start()
+
+        @pl.when(level < z)
+        def _():
+            @pl.when(place.has_up)
+            def _():
+                to_line(level, level, place.down).wait_recv()
+                add(total.at[at], line_in.at[level])
+
+            to_line(level, jnp.where(level == z - 1, depth, level), place.down).start()
+
+    at = slot(place.dp, z)
+
+    @pl.when(place.has_down)
+    def _():
+        to_line(z, z, place.up).wait_recv()
+        add(total.at[at], line_in.at[z])
+
+    @pl.when(place.has_up)
+    def _():
+        to_line(z, depth, place.down).wait_recv()
+        add(total.at[at], line_in.at[depth])
+
+    out_ref[...] = total[at]
+
+    for dp in range(4):
+        for level in levels:
+            to_core(theirs[dp], level).wait_send()
+    for level in levels:
+        to_far(1, place.both_dp, level).wait_send()
+        to_far(0, place.far_dp, level).wait_send()
+        to_near(level).wait_send()
+
+        @pl.when(level != z)
+        def _():
+            to_line(level, level, place.up).wait_send()
+
+
+def reduce_rows(part, depth):
+    blocks, tokens_dev, width = part.shape
+    half = blocks // 2
+
+    def buffer(count):
+        return pltpu.VMEM((count, tokens_dev, width), part.dtype)
+
+    def sems(count):
+        return pltpu.SemaphoreType.DMA((count,))
+
+    return pl.pallas_call(
+        functools.partial(reduce_kernel, depth),
+        out_shape=jax.ShapeDtypeStruct((tokens_dev, width), part.dtype),
+        in_specs=[pl.BlockSpec(memory_space=pl.ANY)],
+        out_specs=pl.BlockSpec(memory_space=pltpu.VMEM),
+        scratch_shapes=[
+            buffer(half),
+            buffer(half),
+            buffer(2 * depth),
+            buffer(depth),
+            buffer(depth + 1),
+            sems(half),
+            sems(half),
+            sems(half),
+            sems(2 * depth),
+            sems(2 * depth),
+            sems(depth),
+            sems(depth),
+            sems(depth),
+            sems(depth + 1),
+        ],
+        compiler_params=pltpu.CompilerParams(
+            collective_id=2, has_side_effects=True, vmem_limit_bytes=60 * 2**20
+        ),
+    )(part)
+
+
 def gathered_mixture(normed, dense_mix, w_gate_up, w_down):
     tokens_dev, experts_all = dense_mix.shape
     hidden_width = w_down.shape[1]
@@ -67,7 +437,8 @@
     capacity = tokens_dev * TOPK // experts_all + 2
     group = 4
     groups, group_rows, group_cap = blocks // group, group * tokens_dev, group * capacity
-    rows_all = lax.all_gather(normed, axes, axis=0, tiled=True)
+    depth = lax.axis_size("ctx") // 2
+    rows_all = gather_rows(normed, depth)
     weights = lax.all_to_all(
         dense_mix.T.reshape(experts_all, 1, tokens_dev), axes, split_axis=0, concat_axis=0, tiled=True
     ).reshape(groups, group_rows)
@@ -96,9 +467,7 @@
         outs.reshape(groups, group_cap, D),
         preferred_element_type=jnp.float32,
     ).astype(jnp.bfloat16)
-    return lax.psum_scatter(
-        part.reshape(blocks * tokens_dev, D), axes, scatter_dimension=0, tiled=True
-    ).astype(jnp.float32)
+    return reduce_rows(part.reshape(blocks, tokens_dev, D), depth).astype(jnp.float32)
 
 
 def shards(
@@ -169,7 +538,7 @@
     chosen = jnp.sum(jnp.where(route_match, logits[:, None, :], 0.0), axis=2)
     gate_values = jax.nn.sigmoid(chosen)
     mixing = gate_values / jnp.sum(gate_values, axis=1, keepdims=True)
-    if experts_all <= 4 * TOPK:
+    if experts_all <= 4 * TOPK and lax.axis_size("dp") == 4 and w_gate_up.shape[0] == 1:
         dense_mix = jnp.sum(jnp.where(route_match, mixing[:, :, None], 0.0), axis=1)
         mixture = gathered_mixture(normed, dense_mix, w_gate_up, w_down)
     else:

time: 666 us -> 439 us (0.66)
  waiting for transfers between devices: 538 us -> 0.02 us
  Pallas kernels: 0 us -> 316 us
    reduce_scatter x1 -> x0, waiting for transfers between devices: 355 us -> none  [gathered_mixture(): lax.psum_scatter(part.reshape(blocks * tokens_dev, D), axes, scatter_dime...]
    pallas_call x0 -> x2, Pallas kernels: none -> 316 us  [the longest x1 169 us: reduce_rows(): pl.pallas_call(functools.partial(reduce_kernel, depth), out_shape=jax.Sha...]
    all_gather x1 -> x0, waiting for transfers between devices: 179 us -> none  [gathered_mixture(): rows_all = lax.all_gather(normed, axes, axis=0, tiled=True)]
  transfers between devices with their start and end apart: 4 -> 2, of which waited for: 3 -> 0; matrix products, arithmetic and copies ran while one was open for 11% -> 18% of each run, Pallas kernels for 0% -> 72%
where the time goes in v2:
time: 439 us; the launch traced here: 438 us
  Pallas kernels  316 us (72%)
  matrix products  71.2 us (16%)
  blocking collectives  16.8 us (4%)
  between operations  14.3 us (3%)
  local copies, waits for them, and re-layouts  7.66 us (2%)
  other arithmetic  7.13 us (2%)
  starting transfers between devices  5.64 us (1%)
    pallas_call x1, Pallas kernels, reduce_rows(): pl.pallas_call(functools.partial(reduce_kernel, depth), out_shape=jax.Sha...  169 us
    pallas_call x1, Pallas kernels, gather_rows(): pl.pallas_call(functools.partial(gather_kernel, depth), out_shape=jax.Sha...  147 us
    dot_general x1, matrix products, gathered_mixture(): jnp.einsum('gct,gcd->gtd', pick, outs.reshape(groups, group_cap, D), pref...  17.3 us
    dot_general x1, matrix products, gathered_mixture(): gate_up = jnp.dot(arrived, w_gate_up[0], preferred_element_type=jnp.float32)  17.3 us
    all_gather x1, blocking collectives, shards(): whole_pairs = lax.all_gather(keys_values, 'ctx', axis=1, tiled=True)  16.8 us
    dot_general x1, matrix products, gathered_mixture(): jnp.einsum('gct,gtd->gcd', pick, rows_all.reshape(groups, group_rows, D),...  16.7 us
    dot_general x1, matrix products, gathered_mixture(): jnp.dot(active, w_down[0], preferred_element_type=jnp.float32)  12.4 us
  transfers between devices with their start and end apart: 2, of which 0 were waited for; matrix products, arithmetic and copies ran while one was open for 18% of the time, Pallas kernels for 72%

profile of v2, /device:TPU:0, one launch (start us, length us, event | category | flops | bytes accessed | tf_op | source)
XLA Modules:
  0.0 438.4 jit_solution(6498656560637149858)
XLA Ops:
  7.2 1.0 reshape.142
  8.3 1.0 reshape.132
  9.4 16.8 %all_gather.3 = bf16[1,1024,256]{2,1,0:T(8,128)(2,1)S(1)} all-gather(bf16[1,128,256]{2,1,0:T(8,128)(2,1)} %param.12), channel_id=1, replica_groups=mesh['dp'=4,'ctx'=8] {'ctx'}, dimensions={1}, use_global_device_ids=true | all-gather | bytes 589824 | tf_op jit(solution)/shard_map/all_gather | solution.py:490
  26.2 0.6 fusion.25
  26.8 0.5 fusion.8
  27.3 0.5 fusion.7
  27.8 0.4 convolution_convert_fusion.3
  28.1 0.5 multiply_reduce_fusion.1
  28.6 0.4 multiply_convert_fusion.1
  29.1 1.0 copy-done.3
  30.1 0.4 fusion.11
  30.5 1.0 copy.35
  31.8 3.1 multiply_reduce_fusion
  34.9 0.3 multiply_convert_fusion.2.rows_ref
  35.2 0.4 fusion.26
  35.8 0.6 select_reduce_fusion.1
  36.4 5.6 %all-to-all-start = ((f32[32,1,128]{2,1,0:T(1,128)}), f32[32,1,128]{2,1,0:T(1,128)S(1)}, u32[]{:S(2)}, u32[]{:S(2)}) async-start(f32[32,1,128]{2,1,0:T(1,128)} %bitcast.6), calls=%async_computation | async-start | bytes 32768 | tf_op jit(solution)/shard_map/all_to_all | solution.py:442
  42.0 1.7 fusion.12
  43.7 146.9 %shard_map.121 = bf16[32,128,4096]{2,1,0:T(8,128)(2,1)} custom-call(bf16[128,4096]{1,0:T(8,128)(2,1)} %copy-done.2), custom_call_target="tpu_custom_call" | custom-call | tf_op jit(solution)/shard_map/pallas_call | solution.py:215
  190.7 0.7 reshape.143
  191.4 0.5 broadcast.109
  191.9 0.7 reduce.5
  192.7 1.3 reduce-window.6
  194.3 0.6 select_reduce_fusion
  195.0 16.7 %convolution_convert_fusion.2 = bf16[8,136,4096]{2,1,0:T(8,128)(2,1)} fusion(bf16[8,512,4096]{2,1,0:T(8,128)(2,1)} %bitcast.54, s32[8,512]{1,0:T(8,128)S(1)} %add_bitcast_fusion, pred[8,512]{1,0:T(8,128)(4,1)S(1)} %broadcast_compare_fusion), kind=kOutput, calls=%fused_computation.5 | convolution fusion | flops 4568973312 | bytes 42487808 | tf_op jit(solution)/shard_map/gct,gtd->gcd/dot_general | solution.py:451
  211.7 17.3 %fusion = f32[1088,1536]{1,0:T(8,128)S(1)} fusion(bf16[1088,4096]{1,0:T(8,128)(2,1)} %bitcast.57, bf16[1,4096,1536]{2,1,0:T(8,128)(2,1)} %param.18), kind=kOutput, calls=%fused_computation.3 | convolution fusion | flops 13690208256 | bytes 28180480 | tf_op jit(solution)/shard_map/dot_general | solution.py:458
  229.0 12.4 %multiply_convert_fusion = bf16[1088,4096]{1,0:T(8,128)(2,1)} fusion(f32[1088]{0:T(1024)S(1)} %mul.73, bf16[1,768,4096]{2,1,0:T(8,128)(2,1)} %param.19, f32[1088,1536]{1,0:T(8,128)S(1)} %fusion), kind=kOutput, calls=%fused_computation.1 | convolution fusion | flops 6867943424 | bytes 21893376 | tf_op jit(solution)/shard_map/dot_general | solution.py:462
  241.4 17.3 %convolution_convert_fusion = bf16[8,512,4096]{2,1,0:T(8,128)(2,1)} fusion(bf16[8,136,4096]{2,1,0:T(8,128)(2,1)} %bitcast.56, s32[8,512]{1,0:T(8,128)S(1)} %add_bitcast_fusion, pred[8,512]{1,0:T(8,128)(4,1)S(1)} %broadcast_compare_fusion), kind=kOutput, calls=%fused_computation | convolution fusion | flops 4581294080 | bytes 42487808 | tf_op jit(solution)/shard_map/gct,gcd->gtd/dot_general | solution.py:464
  258.7 168.7 %shard_map.122 = bf16[128,4096]{1,0:T(8,128)(2,1)} custom-call(bf16[32,128,4096]{2,1,0:T(8,128)(2,1)} %bitcast.55), custom_call_target="tpu_custom_call" | custom-call | tf_op jit(solution)/shard_map/pallas_call | solution.py:405
  427.4 2.4 fusion.17
  429.8 0.9 copy.36
  430.8 0.8 copy.34
  (38 shorter events, 1.0 us)
Async XLA Ops:
  7.2 28.0 %copy-start = (bf16[4096,32]{0,1:T(8,128)(2,1)S(1)}, bf16[4096,32]{0,1:T(8,128)(2,1)}, u32[]{:S(2)}) copy-start(bf16[4096,32]{0,1:T(8,128)(2,1)} %param.16) | copy-start | bytes 786436
  7.2 422.6 %reduce-scatter.4.cloned.1.call-start = ((), (), s32[]{:S(2)}) async-start(), calls=%async_computation.2 | async-start | bytes 589824
  26.2 2.4 copy-start.4
  29.1 1.0 copy-start.3
  30.1 1.7 copy-start.5
  31.8 3.1 copy-start.6
  34.9 0.8 copy-start.7
  35.2 8.5 %copy-start.2 = (bf16[128,4096]{1,0:T(8,128)(2,1)}, bf16[128,4096]{1,0:T(8,128)(2,1)S(1)}, u32[]{:S(2)}) copy-start(bf16[128,4096]{1,0:T(8,128)(2,1)S(1)} %multiply_convert_fusion.2.rows_ref) | copy-start | bytes 3145732
  36.4 155.0 %all-to-all-start = ((f32[32,1,128]{2,1,0:T(1,128)}), f32[32,1,128]{2,1,0:T(1,128)S(1)}, u32[]{:S(2)}, u32[]{:S(2)}) async-start(f32[32,1,128]{2,1,0:T(1,128)} %bitcast.6), calls=%async_computation | async-start | bytes 32768 | tf_op jit(solution)/shard_map/all_to_all | solution.py:442
  258.7 172.9 %copy-start.1 = (bf16[4096,32]{0,1:T(8,128)(2,1)S(1)}, bf16[4096,32]{0,1:T(8,128)(2,1)}, u32[]{:S(2)}) copy-start(bf16[4096,32]{0,1:T(8,128)(2,1)} %param.16) | copy-start | bytes 786436
Sparse Core Ops, SparseCore 0:
  31.6 33.4 reduce-scatter.3

commit v3 on v2

--- a/solution.py
+++ b/solution.py
@@ -106,7 +106,27 @@
         )
 
 
-def gather_kernel(depth, rows_ref, all_ref, own_sem, send_sem, recv_sem):
+def experts_kernel(
+    depth,
+    rows_ref,
+    pick_ref,
+    spread_ref,
+    weight_ref,
+    w_gate_up_ref,
+    w_down_ref,
+    part_ref,
+    all_ref,
+    gate_up_buf,
+    down_buf,
+    plane_rows,
+    arrived,
+    active,
+    own_sem,
+    send_sem,
+    recv_sem,
+    load_sem,
+    weight_sem,
+):
     place = Place(depth)
     z = place.z
     targets = (place.near, place.far, place.other_core, place.up, place.down)
@@ -141,6 +161,12 @@
     pl.when(place.has_down)(lambda: copy(DOWN, own, rows_ref).start())
     for kind in (FAR, NEAR, CORE):
         copy(kind, own, rows_ref).start()
+    weight_copies = (
+        pltpu.make_async_copy(w_gate_up_ref, gate_up_buf, weight_sem.at[0]),
+        pltpu.make_async_copy(w_down_ref, down_buf, weight_sem.at[1]),
+    )
+    weight_copies[0].start()
+    weight_copies[1].start()
 
     def from_line(distance):
         for source, condition, onward in along(distance):
@@ -177,18 +203,80 @@
 
             run(condition, body)
 
+    tokens_dev = rows_ref.shape[0]
+    width, hidden_width = w_gate_up_ref.shape[0], w_down_ref.shape[0]
+
+    def plane_at(turn):
+        outward = lambda at: jnp.where(turn <= at, at - turn, turn)
+        return jnp.where(z < depth // 2, outward(z), depth - 1 - outward(depth - 1 - z))
+
+    def compute(turn):
+        plane = plane_at(turn)
+        for dp in range(4):
+            copy(CORE, place.block(dp, plane, 1 - place.core)).wait_recv()
+        pieces = [
+            (place.block(dp, plane, core), plane_rows.at[pl.ds((dp * 2 + core) * tokens_dev, tokens_dev)])
+            for dp in range(4)
+            for core in range(2)
+        ]
+        loads = [
+            pltpu.make_async_copy(all_ref.at[block], piece, load_sem.at[i])
+            for i, (block, piece) in enumerate(pieces)
+        ]
+        stores = [
+            pltpu.make_async_copy(piece, part_ref.at[block], load_sem.at[i])
+            for i, (block, piece) in enumerate(pieces)
+        ]
+        for load in loads:
+            load.start()
+        for load in loads:
+            load.wait()
+
+        def pick_columns(i, carry):
+            at = pl.ds(pl.multiple_of(i * 512, 512), 512)
+            arrived[:, at] = jnp.dot(
+                pick_ref[plane], plane_rows[:, at], preferred_element_type=jnp.float32
+            ).astype(jnp.bfloat16)
+            return carry
+
+        def up_columns(i, carry):
+            at = pl.ds(pl.multiple_of(i * 256, 256), 256)
+            up_at = pl.ds(pl.multiple_of(hidden_width + i * 256, 256), 256)
+            gate = jnp.dot(arrived[...], gate_up_buf[:, at], preferred_element_type=jnp.float32)
+            up = jnp.dot(arrived[...], gate_up_buf[:, up_at], preferred_element_type=jnp.float32)
+            active[:, at] = (gate / (1.0 + jnp.exp(-gate)) * up).astype(jnp.bfloat16)
+            return carry
+
+        def down_columns(i, carry):
+            at = pl.ds(pl.multiple_of(i * 512, 512), 512)
+            out = jnp.dot(active[...], down_buf[:, at], preferred_element_type=jnp.float32)
+            out = out.astype(jnp.bfloat16).astype(jnp.float32) * weight_ref[plane]
+            plane_rows[:, at] = jnp.dot(
+                spread_ref[plane], out.astype(jnp.bfloat16), preferred_element_type=jnp.float32
+            ).astype(jnp.bfloat16)
+            return carry
+
+        lax.fori_loop(0, width // 512, pick_columns, 0)
+        lax.fori_loop(0, hidden_width // 256, up_columns, 0)
+        lax.fori_loop(0, width // 512, down_columns, 0)
+        for store in stores:
+            store.start()
+        for store in stores:
+            store.wait()
+
     for distance in range(depth):
         if distance:
             from_line(distance)
         from_near(distance)
         if distance:
             from_far(distance - 1)
+            if distance == 1:
+                own_copy.wait()
+                weight_copies[0].wait()
+                weight_copies[1].wait()
+            compute(distance - 1)
     from_far(depth - 1)
-
-    for dp in range(4):
-        for level in range(depth):
-            copy(CORE, place.block(dp, level, 1 - place.core)).wait_recv()
-    own_copy.wait()
+    compute(depth - 1)
     for distance in range(depth):
         for source, condition, onward in along(distance):
 
@@ -209,21 +297,35 @@
             run(condition, body)
 
 
-def gather_rows(rows, depth):
+def gather_and_apply(rows, pick, spread, slot_weight, w_gate_up, w_down, depth):
     tokens_dev, width = rows.shape
     blocks = 8 * depth
-    return pl.pallas_call(
-        functools.partial(gather_kernel, depth),
-        out_shape=jax.ShapeDtypeStruct((blocks, tokens_dev, width), rows.dtype),
-        in_specs=[pl.BlockSpec(memory_space=pl.ANY)],
-        out_specs=pl.BlockSpec(memory_space=pl.ANY),
+    slots, plane_tokens = pick.shape[1:]
+    gathered = jax.ShapeDtypeStruct((blocks, tokens_dev, width), rows.dtype)
+    anywhere = pl.BlockSpec(memory_space=pl.ANY)
+    in_vmem = pl.BlockSpec(memory_space=pltpu.VMEM)
+    part, _ = pl.pallas_call(
+        functools.partial(experts_kernel, depth),
+        out_shape=(gathered, gathered),
+        in_specs=[anywhere, in_vmem, in_vmem, in_vmem, anywhere, anywhere],
+        out_specs=(anywhere, anywhere),
         scratch_shapes=[
+            pltpu.VMEM(w_gate_up.shape, w_gate_up.dtype),
+            pltpu.VMEM(w_down.shape, w_down.dtype),
+            pltpu.VMEM((plane_tokens, width), rows.dtype),
+            pltpu.VMEM((slots, width), rows.dtype),
+            pltpu.VMEM((slots, w_down.shape[0]), rows.dtype),
             pltpu.SemaphoreType.DMA(()),
             pltpu.SemaphoreType.DMA((5, blocks)),
             pltpu.SemaphoreType.DMA((blocks,)),
+            pltpu.SemaphoreType.DMA((8,)),
+            pltpu.SemaphoreType.DMA((2,)),
         ],
-        compiler_params=pltpu.CompilerParams(collective_id=1, has_side_effects=True),
-    )(rows)
+        compiler_params=pltpu.CompilerParams(
+            collective_id=1, has_side_effects=True, vmem_limit_bytes=58 * 2**20
+        ),
+    )(rows, pick, spread, slot_weight, w_gate_up, w_down)
+    return part
 
 
 def reduce_kernel(
@@ -431,43 +533,32 @@
 
 def gathered_mixture(normed, dense_mix, w_gate_up, w_down):
     tokens_dev, experts_all = dense_mix.shape
-    hidden_width = w_down.shape[1]
     axes = ("dp", "ctx")
-    blocks = lax.axis_size("dp") * lax.axis_size("ctx")
+    depth = lax.axis_size("ctx") // 2
     capacity = tokens_dev * TOPK // experts_all + 2
-    group = 4
-    groups, group_rows, group_cap = blocks // group, group * tokens_dev, group * capacity
-    depth = lax.axis_size("ctx") // 2
-    rows_all = gather_rows(normed, depth)
+    slot_count, plane_tokens = 8 * capacity, 8 * tokens_dev
     weights = lax.all_to_all(
         dense_mix.T.reshape(experts_all, 1, tokens_dev), axes, split_axis=0, concat_axis=0, tiled=True
-    ).reshape(groups, group_rows)
+    )
+    weights = (
+        weights.reshape(4, depth, 2, tokens_dev).transpose(1, 0, 2, 3).reshape(depth, plane_tokens)
+    )
     named = weights != 0.0
     rank = jnp.cumsum(named.astype(jnp.int32), axis=1) - 1
-    slots = jnp.arange(group_cap, dtype=jnp.int32)
+    slots = jnp.arange(slot_count, dtype=jnp.int32)
     pick = (rank[:, None, :] == slots[None, :, None]) & named[:, None, :]
-    slot_weight = jnp.sum(jnp.where(pick, weights[:, None, :], 0.0), axis=2)
-    pick = pick.astype(jnp.bfloat16)
-    arrived = jnp.einsum(
-        "gct,gtd->gcd",
-        pick,
-        rows_all.reshape(groups, group_rows, D),
-        preferred_element_type=jnp.float32,
-    ).astype(jnp.bfloat16)
-    arrived = arrived.reshape(groups * group_cap, D)
-    gate_up = jnp.dot(arrived, w_gate_up[0], preferred_element_type=jnp.float32)
-    active = (jax.nn.silu(gate_up[:, :hidden_width]) * gate_up[:, hidden_width:]).astype(
-        jnp.bfloat16
-    )
-    outs = jnp.dot(active, w_down[0], preferred_element_type=jnp.float32).astype(jnp.bfloat16)
-    outs = (outs.astype(jnp.float32) * slot_weight.reshape(-1, 1)).astype(jnp.bfloat16)
-    part = jnp.einsum(
-        "gct,gcd->gtd",
-        pick,
-        outs.reshape(groups, group_cap, D),
-        preferred_element_type=jnp.float32,
-    ).astype(jnp.bfloat16)
-    return reduce_rows(part.reshape(blocks, tokens_dev, D), depth).astype(jnp.float32)
+    slot_weight = jnp.sum(jnp.where(pick, weights[:, None, :], 0.0), axis=2, keepdims=True)
+    spread = (rank[:, :, None] == slots[None, None, :]) & named[:, :, None]
+    part = gather_and_apply(
+        normed,
+        pick.astype(jnp.bfloat16),
+        spread.astype(jnp.bfloat16),
+        slot_weight,
+        w_gate_up[0],
+        w_down[0],
+        depth,
+    )
+    return reduce_rows(part, depth).astype(jnp.float32)
 
 
 def shards(

time: 439 us -> 455 us (1.036)
  Pallas kernels: 316 us -> 381 us
  matrix products: 71.2 us -> 8.44 us
  other arithmetic: 7.13 us -> 12 us
  waiting for transfers between devices: 0.02 us -> 4.68 us
    pallas_call x1, Pallas kernels: 147 us -> 214 us  [gather_and_apply(): pl.pallas_call(functools.partial(experts_kernel, depth), out_shape=(gathe...]
    dot_general x4 -> x0, matrix products: 63.7 us -> none  [the longest x1 17.3 us: gathered_mixture(): jnp.einsum('gct,gcd->gtd', pick, outs.reshape(groups, group_cap, D), pref...]
    convert_element_type x0 -> x2, other arithmetic: none -> 5.11 us  [the longest x1 2.86 us: gathered_mixture(): spread.astype(jnp.bfloat16)]
    all_to_all x1, waiting for transfers between devices: 0.01 us -> 4.66 us  [gathered_mixture(): lax.all_to_all(dense_mix.T.reshape(experts_all, 1, tokens_dev), axes, spl...]
  transfers between devices with their start and end apart: 2 -> 2, of which waited for: 0 -> 1; matrix products, arithmetic and copies ran while one was open for 18% -> 4% of each run, Pallas kernels for 72% -> 85%
where the time goes in v3:
time: 455 us; the launch traced here: 451 us
  Pallas kernels  381 us (84%)
  blocking collectives  16.8 us (4%)
  between operations  14.3 us (3%)
  other arithmetic  12 us (3%)
  matrix products  8.44 us (2%)
  local copies, waits for them, and re-layouts  7.65 us (2%)
  starting transfers between devices  5.64 us (1%)
  waiting for transfers between devices  4.68 us (1%)
    pallas_call x1, Pallas kernels, gather_and_apply(): pl.pallas_call(functools.partial(experts_kernel, depth), out_shape=(gathe...  214 us
    pallas_call x1, Pallas kernels, reduce_rows(): pl.pallas_call(functools.partial(reduce_kernel, depth), out_shape=jax.Sha...  167 us
    all_gather x1, blocking collectives, shards(): whole_pairs = lax.all_gather(keys_values, 'ctx', axis=1, tiled=True)  16.8 us
  transfers between devices with their start and end apart: 2, of which 1 were waited for; matrix products, arithmetic and copies ran while one was open for 4% of the time, Pallas kernels for 85%

profile of v3, /device:TPU:0, one launch (start us, length us, event | category | flops | bytes accessed | tf_op | source)
XLA Modules:
  0.0 450.6 jit_solution(2338430363704302491)
XLA Ops:
  7.2 1.0 reshape.143
  8.3 1.0 reshape.136
  9.4 16.8 %all_gather.3 = bf16[1,1024,256]{2,1,0:T(8,128)(2,1)S(1)} all-gather(bf16[1,128,256]{2,1,0:T(8,128)(2,1)} %param.12), channel_id=1, replica_groups=mesh['dp'=4,'ctx'=8] {'ctx'}, dimensions={1}, use_global_device_ids=true | all-gather | bytes 589824 | tf_op jit(solution)/shard_map/all_gather | solution.py:581
  26.2 0.6 fusion.15
  26.8 0.5 fusion.5
  27.3 0.5 fusion.4
  27.8 0.3 convolution_convert_fusion
  28.1 1.2 multiply_reduce_fusion.1
  29.3 0.4 multiply_convert_fusion
  29.8 0.4 copy-done.7
  30.2 0.4 fusion.6
  30.6 1.0 copy.53
  31.9 3.4 multiply_reduce_fusion
  35.3 0.3 multiply_convert_fusion.1.rows_ref
  35.6 0.4 fusion.16
  36.2 0.6 select_reduce_fusion.1
  36.8 5.6 %all-to-all-start = ((f32[32,1,128]{2,1,0:T(1,128)}), f32[32,1,128]{2,1,0:T(1,128)S(1)}, u32[]{:S(2)}, u32[]{:S(2)}) async-start(f32[32,1,128]{2,1,0:T(1,128)} %bitcast.6), calls=%async_computation | async-start | bytes 32768 | tf_op jit(solution)/shard_map/all_to_all | solution.py:540
  42.4 1.7 fusion.7
  44.1 0.7 reshape.144
  44.9 4.7 %all-to-all-done = f32[32,1,128]{2,1,0:T(1,128)S(1)} async-done(((f32[32,1,128]{2,1,0:T(1,128)}), f32[32,1,128]{2,1,0:T(1,128)S(1)}, u32[]{:S(2)}, u32[]{:S(2)}) %all-to-all-start) | async-done | bytes 16416 | tf_op jit(solution)/shard_map/all_to_all | solution.py:540
  49.6 1.1 reduce-window.6
  50.8 0.2 slice_reduce_fusion
  51.0 0.2 reduce-window.9
  51.3 2.3 fusion.3.pick_ref
  53.5 2.9 fusion.1.spread_ref
  56.4 1.1 select_reduce_fusion
  57.5 1.1 copy.50.weight_ref
  58.5 214.4 %shard_map.121 = (bf16[32,128,4096]{2,1,0:T(8,128)(2,1)}, bf16[32,128,4096]{2,1,0:T(8,128)(2,1)}) custom-call(bf16[128,4096]{1,0:T(8,128)(2,1)} %copy-done.2, bf16[4,272,1024]{2,1,0:T(8,128)(2,1)} %fusion.3.pick_ref, bf16[4,1024,272]{2,1,0:T(8,128)(2,1)} %fusion.1.spread_ref, f32[4,272,1]{2,1,0:T(8,128)} %copy.50.weight_ref, bf16[4096,1536]{1,0:T(8,128)(2,1)} %bitcast.53, ...), custom_call_target="tpu_custom_call" | custom-call | tf_op jit(solution)/shard_map/pallas_call | solution.py:307
  272.9 166.7 %shard_map.122 = bf16[128,4096]{1,0:T(8,128)(2,1)} custom-call(bf16[32,128,4096]{2,1,0:T(8,128)(2,1)} %get-tuple-element.4.part_ref), custom_call_target="tpu_custom_call" | custom-call | tf_op jit(solution)/shard_map/pallas_call | solution.py:507
  439.6 2.4 fusion.8
  442.0 0.9 copy.54
  443.0 0.8 copy.52
  (40 shorter events, 0.7 us)
Async XLA Ops:
  7.2 28.5 %copy-start = (bf16[4096,32]{0,1:T(8,128)(2,1)S(1)}, bf16[4096,32]{0,1:T(8,128)(2,1)}, u32[]{:S(2)}) copy-start(bf16[4096,32]{0,1:T(8,128)(2,1)} %param.16) | copy-start | bytes 786436
  7.2 434.9 %reduce-scatter.4.cloned.1.call-start = ((), (), s32[]{:S(2)}) async-start(), calls=%async_computation.2 | async-start | bytes 589824
  9.3 18.0 %copy-start.6 = (bf16[512,128]{1,0:T(8,128)(2,1)}, bf16[512,128]{1,0:T(8,128)(2,1)S(1)}, u32[]{:S(2)}) copy-start(bf16[512,128]{1,0:T(8,128)(2,1)S(1)} %reshape.136) | copy-start | bytes 393220
  26.2 3.1 copy-start.4
  29.3 0.9 copy-start.7
  30.2 5.1 %copy-start.3 = (bf16[512,1024]{1,0:T(8,128)(2,1)}, bf16[512,1024]{1,0:T(8,128)(2,1)S(1)}, u32[]{:S(2)}) copy-start(bf16[512,1024]{1,0:T(8,128)(2,1)S(1)} %multiply_convert_fusion) | copy-start | bytes 3145732
  30.2 1.4 copy-start.5
  31.9 3.4 copy-start.8
  35.3 0.8 copy-start.9
  35.6 17.9 %copy-start.2 = (bf16[128,4096]{1,0:T(8,128)(2,1)}, bf16[128,4096]{1,0:T(8,128)(2,1)S(1)}, u32[]{:S(2)}) copy-start(bf16[128,4096]{1,0:T(8,128)(2,1)S(1)} %multiply_convert_fusion.1.rows_ref) | copy-start | bytes 3145732
  36.8 12.7 %all-to-all-start = ((f32[32,1,128]{2,1,0:T(1,128)}), f32[32,1,128]{2,1,0:T(1,128)S(1)}, u32[]{:S(2)}, u32[]{:S(2)}) async-start(f32[32,1,128]{2,1,0:T(1,128)} %bitcast.6), calls=%async_computation | async-start | bytes 32768 | tf_op jit(solution)/shard_map/all_to_all | solution.py:540
  272.9 170.8 %copy-start.1 = (bf16[4096,32]{0,1:T(8,128)(2,1)S(1)}, bf16[4096,32]{0,1:T(8,128)(2,1)}, u32[]{:S(2)}) copy-start(bf16[4096,32]{0,1:T(8,128)(2,1)} %param.16) | copy-start | bytes 786436
Sparse Core Ops, SparseCore 0:
  31.7 32.1 reduce-scatter.3

commit v4 on v3

--- a/solution.py
+++ b/solution.py
@@ -268,15 +268,15 @@
         if distance:
             from_line(distance)
         from_near(distance)
-        if distance:
-            from_far(distance - 1)
-            if distance == 1:
-                own_copy.wait()
-                weight_copies[0].wait()
-                weight_copies[1].wait()
-            compute(distance - 1)
-    from_far(depth - 1)
-    compute(depth - 1)
+        if distance > 1:
+            from_far(distance - 2)
+    own_copy.wait()
+    weight_copies[0].wait()
+    weight_copies[1].wait()
+    for turn in range(depth):
+        if turn >= depth - 2:
+            from_far(turn)
+        compute(turn)
     for distance in range(depth):
         for source, condition, onward in along(distance):
 
@@ -425,24 +425,31 @@
     place.greet()
     theirs = (place.both_dp, place.near_dp, place.far_dp, place.dp)
     mine = (place.both_dp, place.far_dp, place.near_dp, place.dp)
-    for dp in range(4):
+    for half in ((0, 1), (2, 3)):
         for level in levels:
-            to_core(theirs[dp], level).start()
-            load(mine[dp], level).start()
-    for turn, dp in enumerate(mine):
+            for turn in half:
+                to_core(theirs[turn], level).start()
+                load(mine[turn], level).start()
+    for half in ((0, 1), (2, 3)):
         for level in levels:
-            at = slot(dp, level)
-            load(dp, level).wait()
-            to_core(dp, level).wait_recv()
-            add(total.at[at], core_in.at[at])
-            if turn < 2:
-                to_far(1 - turn, dp, level).start()
-    for level in levels:
+            for turn in half:
+                at = slot(mine[turn], level)
+                load(mine[turn], level).wait()
+                to_core(mine[turn], level).wait_recv()
+                add(total.at[at], core_in.at[at])
+                if turn < 2:
+                    to_far(1 - turn, mine[turn], level).start()
+
+    def pass_near(level):
         at = slot(place.near_dp, level)
         to_far(1, place.both_dp, level).wait_recv()
         add(total.at[at], far_in.at[depth + level])
         to_near(level).start()
-    for level in levels:
+
+    pass_near(levels[0])
+    for i, level in enumerate(levels):
+        if i + 1 < depth:
+            pass_near(levels[i + 1])
         at = slot(place.dp, level)
         to_far(0, place.far_dp, level).wait_recv()
         add(total.at[at], far_in.at[level])

time: 455 us -> 440 us (0.967)
  Pallas kernels: 381 us -> 369 us
    pallas_call x1, Pallas kernels: 167 us -> 145 us  [reduce_rows(): pl.pallas_call(functools.partial(reduce_kernel, depth), out_shape=jax.Sha...]
    pallas_call x1, Pallas kernels: 214 us -> 224 us  [gather_and_apply(): pl.pallas_call(functools.partial(experts_kernel, depth), out_shape=(gathe...]
  transfers between devices with their start and end apart: 2 -> 2, of which waited for: 1 -> 1; matrix products, arithmetic and copies ran while one was open for 4% -> 4% of each run, Pallas kernels for 85% -> 84%
where the time goes in v4:
time: 440 us; the launch traced here: 438 us
  Pallas kernels  369 us (84%)
  blocking collectives  16.8 us (4%)
  between operations  14.3 us (3%)
  other arithmetic  12 us (3%)
  matrix products  8.44 us (2%)
  local copies, waits for them, and re-layouts  7.65 us (2%)
  starting transfers between devices  5.64 us (1%)
  waiting for transfers between devices  4.68 us (1%)
    pallas_call x1, Pallas kernels, gather_and_apply(): pl.pallas_call(functools.partial(experts_kernel, depth), out_shape=(gathe...  224 us
    pallas_call x1, Pallas kernels, reduce_rows(): pl.pallas_call(functools.partial(reduce_kernel, depth), out_shape=jax.Sha...  145 us
    all_gather x1, blocking collectives, shards(): whole_pairs = lax.all_gather(keys_values, 'ctx', axis=1, tiled=True)  16.8 us
  transfers between devices with their start and end apart: 2, of which 1 were waited for; matrix products, arithmetic and copies ran while one was open for 4% of the time, Pallas kernels for 84%

profile of v4, /device:TPU:0, one launch (start us, length us, event | category | flops | bytes accessed | tf_op | source)
XLA Modules:
  0.0 438.4 jit_solution(5159078539302447748)
XLA Ops:
  7.2 1.0 reshape.143
  8.3 1.0 reshape.136
  9.4 16.8 %all_gather.3 = bf16[1,1024,256]{2,1,0:T(8,128)(2,1)S(1)} all-gather(bf16[1,128,256]{2,1,0:T(8,128)(2,1)} %param.12), channel_id=1, replica_groups=mesh['dp'=4,'ctx'=8] {'ctx'}, dimensions={1}, use_global_device_ids=true | all-gather | bytes 589824 | tf_op jit(solution)/shard_map/all_gather | solution.py:588
  26.2 0.6 fusion.15
  26.8 0.5 fusion.5
  27.3 0.5 fusion.4
  27.8 0.3 convolution_convert_fusion
  28.1 1.2 multiply_reduce_fusion.1
  29.3 0.4 multiply_convert_fusion
  29.8 0.4 copy-done.7
  30.2 0.4 fusion.6
  30.6 1.0 copy.53
  31.9 3.4 multiply_reduce_fusion
  35.3 0.3 multiply_convert_fusion.1.rows_ref
  35.6 0.4 fusion.16
  36.2 0.6 select_reduce_fusion.1
  36.8 5.6 %all-to-all-start = ((f32[32,1,128]{2,1,0:T(1,128)}), f32[32,1,128]{2,1,0:T(1,128)S(1)}, u32[]{:S(2)}, u32[]{:S(2)}) async-start(f32[32,1,128]{2,1,0:T(1,128)} %bitcast.6), calls=%async_computation | async-start | bytes 32768 | tf_op jit(solution)/shard_map/all_to_all | solution.py:547
  42.4 1.7 fusion.7
  44.1 0.7 reshape.144
  44.9 4.7 %all-to-all-done = f32[32,1,128]{2,1,0:T(1,128)S(1)} async-done(((f32[32,1,128]{2,1,0:T(1,128)}), f32[32,1,128]{2,1,0:T(1,128)S(1)}, u32[]{:S(2)}, u32[]{:S(2)}) %all-to-all-start) | async-done | bytes 16416 | tf_op jit(solution)/shard_map/all_to_all | solution.py:547
  49.6 1.1 reduce-window.6
  50.8 0.2 slice_reduce_fusion
  51.0 0.2 reduce-window.9
  51.3 2.3 fusion.3.pick_ref
  53.5 2.9 fusion.1.spread_ref
  56.4 1.1 select_reduce_fusion
  57.5 1.1 copy.50.weight_ref
  58.5 224.2 %shard_map.121 = (bf16[32,128,4096]{2,1,0:T(8,128)(2,1)}, bf16[32,128,4096]{2,1,0:T(8,128)(2,1)}) custom-call(bf16[128,4096]{1,0:T(8,128)(2,1)} %copy-done.2, bf16[4,272,1024]{2,1,0:T(8,128)(2,1)} %fusion.3.pick_ref, bf16[4,1024,272]{2,1,0:T(8,128)(2,1)} %fusion.1.spread_ref, f32[4,272,1]{2,1,0:T(8,128)} %copy.50.weight_ref, bf16[4096,1536]{1,0:T(8,128)(2,1)} %bitcast.53, ...), custom_call_target="tpu_custom_call" | custom-call | tf_op jit(solution)/shard_map/pallas_call | solution.py:307
  282.8 144.7 %shard_map.122 = bf16[128,4096]{1,0:T(8,128)(2,1)} custom-call(bf16[32,128,4096]{2,1,0:T(8,128)(2,1)} %get-tuple-element.4.part_ref), custom_call_target="tpu_custom_call" | custom-call | tf_op jit(solution)/shard_map/pallas_call | solution.py:514
  427.4 2.4 fusion.8
  429.9 0.9 copy.54
  430.8 0.8 copy.52
  (40 shorter events, 0.7 us)
Async XLA Ops:
  7.2 28.5 %copy-start = (bf16[4096,32]{0,1:T(8,128)(2,1)S(1)}, bf16[4096,32]{0,1:T(8,128)(2,1)}, u32[]{:S(2)}) copy-start(bf16[4096,32]{0,1:T(8,128)(2,1)} %param.16) | copy-start | bytes 786436
  7.2 422.7 %reduce-scatter.4.cloned.1.call-start = ((), (), s32[]{:S(2)}) async-start(), calls=%async_computation.2 | async-start | bytes 589824
  9.3 18.0 %copy-start.6 = (bf16[512,128]{1,0:T(8,128)(2,1)}, bf16[512,128]{1,0:T(8,128)(2,1)S(1)}, u32[]{:S(2)}) copy-start(bf16[512,128]{1,0:T(8,128)(2,1)S(1)} %reshape.136) | copy-start | bytes 393220
  26.2 3.1 copy-start.4
  29.3 0.9 copy-start.7
  30.2 5.1 %copy-start.3 = (bf16[512,1024]{1,0:T(8,128)(2,1)}, bf16[512,1024]{1,0:T(8,128)(2,1)S(1)}, u32[]{:S(2)}) copy-start(bf16[512,1024]{1,0:T(8,128)(2,1)S(1)} %multiply_convert_fusion) | copy-start | bytes 3145732
  30.2 1.4 copy-start.5
  31.9 3.4 copy-start.8
  35.3 0.8 copy-start.9
  35.6 17.9 %copy-start.2 = (bf16[128,4096]{1,0:T(8,128)(2,1)}, bf16[128,4096]{1,0:T(8,128)(2,1)S(1)}, u32[]{:S(2)}) copy-start(bf16[128,4096]{1,0:T(8,128)(2,1)S(1)} %multiply_convert_fusion.1.rows_ref) | copy-start | bytes 3145732
  36.8 12.7 %all-to-all-start = ((f32[32,1,128]{2,1,0:T(1,128)}), f32[32,1,128]{2,1,0:T(1,128)S(1)}, u32[]{:S(2)}, u32[]{:S(2)}) async-start(f32[32,1,128]{2,1,0:T(1,128)} %bitcast.6), calls=%async_computation | async-start | bytes 32768 | tf_op jit(solution)/shard_map/all_to_all | solution.py:547
  282.7 148.8 %copy-start.1 = (bf16[4096,32]{0,1:T(8,128)(2,1)S(1)}, bf16[4096,32]{0,1:T(8,128)(2,1)}, u32[]{:S(2)}) copy-start(bf16[4096,32]{0,1:T(8,128)(2,1)} %param.16) | copy-start | bytes 786436
Sparse Core Ops, SparseCore 0:
  31.7 32.1 reduce-scatter.3
